TPU v7x, 512 devices: a whole 4x4x16 slice. The times are simulated.
512 devices in a mesh: seq: 128 (over x, z, core), head: 4 (over y).
Axes of the slice: x: 4, y: 4, z: 16, core: 2. Of those that a mesh axis runs over, the one named last changes fastest.
Arguments:
- query_rot: bfloat16 [16384, 2048], P('seq', 'head'), may hold values from -6 to 6
- key_rot: bfloat16 [16384, 2048], P('seq', 'head'), may hold values from -6 to 6
- value_rot: bfloat16 [16384, 2048], P('seq', 'head'), may hold values from -6 to 6
- grad_out: bfloat16 [16384, 2048], P(('seq', 'head')), may hold values from -6 to 6
Outputs:
- attn_out: bfloat16 [16384, 2048], P(('seq', 'head'))
- grad_query: bfloat16 [16384, 2048], P('seq', 'head')
- grad_key: bfloat16 [16384, 2048], P('seq', 'head')
- grad_value: bfloat16 [16384, 2048], P('seq', 'head')
All inputs are finite; a program needn't handle non-finite values.
Results may differ from a plain program's by a relative error of at most 0.0058.
Values may be sent and summed in bfloat16 or wider, within the bound.
A program may use at most 192 MiB of HBM per device.

v0:
```python
import jax
import jax.numpy as jnp
from jax import lax
from jax.sharding import PartitionSpec as P

DH = 64
GROUP = 128


def prefix(part, axis, combine, identity, reverse):
    count = lax.axis_size(axis)
    place = lax.axis_index(axis)
    ahead = count - 1 - place if reverse else place
    gathered = lax.all_gather(part, axis)
    state = jnp.zeros_like(part) + jnp.asarray(identity, part.dtype)

    def one(step, state):
        source = count - 1 - step if reverse else step
        return combine(state, lax.dynamic_index_in_dim(gathered, source, 0, False))

    return lax.fori_loop(0, ahead, one, state)


def add_states(earlier, later):
    return earlier + later


def masked(causal, left, right):
    products = jnp.einsum("cthd,cshd->chts", left, right, preferred_element_type=jnp.float32)
    return jnp.where(causal, products, 0.0).astype(jnp.bfloat16)


def shards(query_rot, key_rot, value_rot, grad_out):
    grad_local = lax.all_to_all(grad_out, "head", split_axis=1, concat_axis=0, tiled=True)
    tok_rows = query_rot.shape[0]
    head_count = query_rot.shape[1] // DH
    blocks = tok_rows // GROUP
    offset = lax.axis_index("seq") * tok_rows
    positions = (offset + jnp.arange(tok_rows, dtype=jnp.int32)).astype(jnp.float32)
    factor = 1.0 / jnp.sqrt(DH * (positions + 1.0))
    scaled_query = (query_rot.astype(jnp.float32) * factor[:, None]).astype(jnp.bfloat16)
    scaled_grad = (grad_local.astype(jnp.float32) * factor[:, None]).astype(jnp.bfloat16)
    shape_four = (blocks, GROUP, head_count, DH)
    query_blocks = query_rot.reshape(shape_four)
    key_blocks = key_rot.reshape(shape_four)
    value_blocks = value_rot.reshape(shape_four)
    squery_blocks = scaled_query.reshape(shape_four)
    sgrad_blocks = scaled_grad.reshape(shape_four)
    local_kv = jnp.einsum(
        "cshd,cshe->chde", key_blocks, value_blocks, preferred_element_type=jnp.float32
    )
    local_qg = jnp.einsum(
        "cthd,cthe->chde", query_blocks, sgrad_blocks, preferred_element_type=jnp.float32
    )
    kv_total = jnp.sum(local_kv, axis=0)
    qg_total = jnp.sum(local_qg, axis=0)
    empty_state = jnp.zeros_like(kv_total)
    earlier_sum = prefix(kv_total, "seq", add_states, empty_state, False)
    later_sum = prefix(qg_total, "seq", add_states, empty_state, True)
    kv_state = earlier_sum[None] + jnp.cumsum(local_kv, axis=0) - local_kv
    grad_state = later_sum[None] + jnp.flip(jnp.cumsum(jnp.flip(local_qg, 0), axis=0), 0) - local_qg
    kv_round = kv_state.astype(jnp.bfloat16)
    grad_round = grad_state.astype(jnp.bfloat16)
    causal = jnp.tril(jnp.ones((GROUP, GROUP), jnp.bool_))
    scores = masked(causal, squery_blocks, key_blocks)
    grad_scores = masked(causal, sgrad_blocks, value_blocks)
    plain_scores = masked(causal, query_blocks, key_blocks)
    attended = jnp.einsum(
        "chts,cshd->cthd", scores, value_blocks, preferred_element_type=jnp.float32
    )
    attended = attended + jnp.einsum(
        "cthd,chde->cthe", squery_blocks, kv_round, preferred_element_type=jnp.float32
    )
    grad_query = jnp.einsum(
        "chts,cshd->cthd", grad_scores, key_blocks, preferred_element_type=jnp.float32
    )
    grad_query = grad_query + jnp.einsum(
        "cthe,chde->cthd", sgrad_blocks, kv_round, preferred_element_type=jnp.float32
    )
    grad_key = jnp.einsum(
        "chts,cthd->cshd", grad_scores, query_blocks, preferred_element_type=jnp.float32
    )
    grad_key = grad_key + jnp.einsum(
        "cshe,chde->cshd", value_blocks, grad_round, preferred_element_type=jnp.float32
    )
    grad_value = jnp.einsum(
        "chts,cthe->cshe", plain_scores, sgrad_blocks, preferred_element_type=jnp.float32
    )
    grad_value = grad_value + jnp.einsum(
        "csha,chae->cshe", key_blocks, grad_round, preferred_element_type=jnp.float32
    )
    width = head_count * DH
    attn_local = attended.astype(jnp.bfloat16).reshape(tok_rows, width)
    attn_out = lax.all_to_all(attn_local, "head", split_axis=0, concat_axis=1, tiled=True)
    return (
        attn_out,
        grad_query.astype(jnp.bfloat16).reshape(tok_rows, width),
        grad_key.astype(jnp.bfloat16).reshape(tok_rows, width),
        grad_value.astype(jnp.bfloat16).reshape(tok_rows, width),
    )


def solution(mesh):
    in_specs = (P("seq", "head"), P("seq", "head"), P("seq", "head"), P(("seq", "head"), None))
    out_specs = (P(("seq", "head"), None), P("seq", "head"), P("seq", "head"), P("seq", "head"))
    return jax.shard_map(shards, mesh=mesh, in_specs=in_specs, out_specs=out_specs, check_vma=False)
```

profile of v0, /device:TPU:1, one launch (start us, length us, event | category | flops | bytes accessed | tf_op | source)
XLA Modules:
  0.0 546.9 jit_solution(13292311088811374999)
XLA Ops:
  7.2 1.0 copy.82
  8.2 1.0 copy.81
  10.2 1.6 copy.100
  11.8 5.0 all-to-all-start.1
  16.8 1.0 copy.80
  17.8 3.8 all-to-all-done.1
  24.6 187.4 %all-gather.5.cloned.1.call-done = f32[1024,64,64]{2,1,0:T(8,128)} async-done(((f32[8,64,64]{2,1,0:T(8,128)}), f32[1024,64,64]{2,1,0:T(8,128)}) %all-gather.5.cloned.1.call-update) | async-done | bytes 16777232 | tf_op jit(solution)/shard_map/all_gather | solution.py:14
  212.1 1.0 while.22
  212.1 1.0 bitcast_add_fusion.4
  215.4 4.0 all-to-all-start
  220.3 4.8 all-to-all-done
  225.8 181.0 %all-gather.7.cloned.1.call-done = f32[1024,64,64]{2,1,0:T(8,128)} async-done(((f32[8,64,64]{2,1,0:T(8,128)}), f32[1024,64,64]{2,1,0:T(8,128)}) %all-gather.7.cloned.1.call-update) | async-done | bytes 16777232 | tf_op jit(solution)/shard_map/all_gather | solution.py:14
  406.8 130.9 %while.23 = (s32[]{:T(128)}, f32[8,64,64]{2,1,0:T(8,128)S(1)}, s32[]{:T(128)}, f32[128,8,64,64]{3,2,1,0:T(8,128)}, s32[]{:T(128)}, /*index=5*/s32[]{:T(128)}, s32[]{:T(128)}, s32[]{:T(128)}) while((s32[]{:T(128)}, f32[8,64,64]{2,1,0:T(8,128)S(1)}, s32[]{:T(128)}, f32[128,8,64,64]{3,2,1,0:T(8,128)}, s32[]{:T(128)}, /*index=5*/s32[]{:T(128)}, ...), condition=%wide.region_3.4_spmd, body=%wide.region_2.3_spmd.sunk | while | flops 32774 | bytes 393359 | solution.py:21
  406.8 1.0 bitcast_add_fusion.5
  408.9 1.0 bitcast_add_fusion.5
  409.9 1.0 bitcast_add_fusion.5
  411.0 1.0 bitcast_add_fusion.5
  412.0 1.0 bitcast_add_fusion.5
  413.1 1.0 bitcast_add_fusion.5
  414.1 1.0 bitcast_add_fusion.5
  415.1 1.0 bitcast_add_fusion.5
  417.2 1.0 bitcast_add_fusion.5
  418.3 1.0 bitcast_add_fusion.5
  420.3 1.0 bitcast_add_fusion.5
  421.4 1.0 bitcast_add_fusion.5
  422.4 1.0 bitcast_add_fusion.5
  423.5 1.0 bitcast_add_fusion.5
  425.5 1.0 bitcast_add_fusion.5
  426.6 1.0 bitcast_add_fusion.5
  428.7 1.0 bitcast_add_fusion.5
  429.7 1.0 bitcast_add_fusion.5
  430.7 1.0 bitcast_add_fusion.5
  431.8 1.0 bitcast_add_fusion.5
  432.8 1.0 bitcast_add_fusion.5
  433.8 1.0 bitcast_add_fusion.5
  434.9 1.0 bitcast_add_fusion.5
  437.0 1.0 bitcast_add_fusion.5
  438.0 1.0 bitcast_add_fusion.5
  440.1 1.0 bitcast_add_fusion.5
  441.1 1.0 bitcast_add_fusion.5
  442.2 1.0 bitcast_add_fusion.5
  443.2 1.0 bitcast_add_fusion.5
  445.3 1.0 bitcast_add_fusion.5
  446.3 1.0 bitcast_add_fusion.5
  448.4 1.0 bitcast_add_fusion.5
  449.4 1.0 bitcast_add_fusion.5
  450.5 1.0 bitcast_add_fusion.5
  451.5 1.0 bitcast_add_fusion.5
  (125 shorter events, 102.6 us)
Async XLA Ops:
  7.2 204.9 %all-gather.5.cloned.1.call-start = ((), (), s32[]{:S(2)}) async-start(), calls=%async_computation.2 | async-start | bytes 33816576 | tf_op jit(solution)/shard_map/all_gather | solution.py:14
  11.8 9.8 %all-to-all-start.1 = ((bf16[32,4,512]{2,0,1:T(8,128)(2,1)}), bf16[32,4,512]{2,0,1:T(8,128)(2,1)S(1)}, u32[]{:S(2)}, u32[]{:S(2)}) async-start(bf16[32,4,512]{2,0,1:T(8,128)(2,1)} %bitcast.75), calls=%async_computation.1 | async-start | bytes 262144 | tf_op jit(solution)/shard_map/all_to_all | solution.py:34
  16.8 390.0 %all-gather.7.cloned.1.call-start = ((), (), s32[]{:S(2)}) async-start(), calls=%async_computation.3 | async-start | bytes 33816576 | tf_op jit(solution)/shard_map/all_gather | solution.py:14
  215.4 9.7 %all-to-all-start = ((bf16[4,32,512]{2,1,0:T(8,128)(2,1)}), bf16[4,32,512]{2,1,0:T(8,128)(2,1)S(1)}, u32[]{:S(2)}, u32[]{:S(2)}) async-start(bf16[4,32,512]{2,1,0:T(8,128)(2,1)} %all_to_all.24), calls=%async_computation | async-start | bytes 262144 | tf_op jit(solution)/shard_map/all_to_all | solution.py:94
Sparse Core Ops, SparseCore 0:
  11.1 200.8 all-gather.4
  215.2 191.5 all-gather.6
where the time goes:
time: 551 us; the launch traced here: 547 us
  waiting for transfers between devices  377 us (68%)
  other arithmetic  130 us (24%)
  between operations  14.2 us (3%)
  local copies, waits for them, and re-layouts  10 us (2%)
  starting transfers between devices  9.05 us (2%)
    all_gather x2, waiting for transfers between devices, prefix(): gathered = lax.all_gather(part, axis)  368 us
    add x127, other arithmetic, add_states(): return earlier + later  129 us
  transfers between devices with their start and end apart: 4, of which 4 were waited for; matrix products, arithmetic and copies ran while one was open for 2% of the time, Pallas kernels for 0%

commit v1 on v0

v1 whole, which is shorter than its diff:
```python
import functools

import jax
import jax.numpy as jnp
from jax import lax
from jax.experimental import pallas as pl
from jax.experimental.pallas import tpu as pltpu
from jax.sharding import PartitionSpec as P

DH = 64
GROUP = 128
XS = 4
ZS = 16
CORES = 2
PAIR = 2 * DH
HALF = DH // CORES
MESH = pl.DeviceIdType.MESH
F32 = jnp.float32
BF16 = jnp.bfloat16

NN = (((1,), (0,)), ((), ()))
NT = (((1,), (1,)), ((), ()))
TN = (((0,), (0,)), ((), ()))


def dot(a, b, dims=NN):
    return lax.dot_general(a, b, dims, preferred_element_type=F32)


def iota(shape, dim):
    return lax.broadcasted_iota(jnp.int32, shape, dim)


def kernel(
    xs, zs, ys,
    q_hbm, k_hbm, v_hbm, g_hbm,
    attn_o, gq_o, gk_o, gv_o,
    q, k, v, g,
    state_f, state_r,
    part_f, part_r,
    chip_f, chip_r,
    line, line_out,
    scan_f, scan_r,
    full_f, full_r,
    kv, gr,
    attn_l, gq_l, gk_l, gv_l,
    attn_s, attn_r, gq_s, gk_s, gv_s,
    perm_in, perm_out, order,
    in_sem, out_sem, send_sem, recv_sem,
):
    columns = xs * CORES
    owners = zs // 2
    sub = HALF // owners
    chunk = xs * sub
    width = q.shape[1]
    pairs = width // PAIR
    rows_y = GROUP // ys

    seq = lax.axis_index("seq")
    y = lax.axis_index("head")
    x = seq // (zs * CORES)
    z = (seq // CORES) % zs
    core = seq % CORES
    column = x * CORES + core
    even = z % 2 == 0

    def at_column(o):
        return (((o // CORES) * zs + z) * CORES + o % CORES, y)

    def at_z(zz):
        return ((x * zs + zz) * CORES + core, y)

    def at_y(yy):
        return (seq, yy)

    def rows(i, n):
        return pl.ds(pl.multiple_of(i * n, n), n)

    def cols(i, n):
        return pl.ds(pl.multiple_of(i * n, n), n)

    def send(src, dst, which, device):
        pltpu.make_async_remote_copy(
            src_ref=src, dst_ref=dst, send_sem=send_sem.at[which], recv_sem=recv_sem.at[which],
            device_id=device, device_id_type=MESH,
        ).start()

    def arrived(ref, which):
        pltpu.make_async_copy(ref, ref, recv_sem.at[which]).wait()

    def sent(ref, which):
        pltpu.make_async_copy(ref, ref, send_sem.at[which]).wait()

    G, P1F, P1R, P2, P3F, P3R, P4F, P4R, AT = range(9)

    loads = [
        pltpu.make_async_copy(src, dst, in_sem.at[i])
        for i, (src, dst) in enumerate(
            (
                (k_hbm, k), (v_hbm, v), (q_hbm, q),
                (g_hbm.at[:, cols(y, width)], g.at[rows(y, rows_y)]),
            )
        )
    ]
    for load in loads:
        load.start()

    barrier = pltpu.get_barrier_semaphore()
    peers = []
    for d in range(1, ys):
        peers.append(at_y((y + d) % ys))
    for d in range(1, columns):
        peers.append(at_column((column + d) % columns))
    for d in range(1, zs):
        peers.append(at_z((z + d) % zs))
    for peer in peers:
        pl.semaphore_signal(barrier, inc=1, device_id=peer, device_id_type=MESH)

    lane_low = iota((GROUP, PAIR), 1) < DH
    state_low = iota((DH, PAIR), 1) < DH

    def split(a):
        return jnp.concatenate([jnp.where(lane_low, a, 0), jnp.where(lane_low, 0, a)], axis=0)

    def beside(a):
        return jnp.concatenate([a[:GROUP], a[GROUP:]], axis=1)

    def diagonal(s):
        return jnp.concatenate([jnp.where(state_low, s, 0), jnp.where(state_low, 0, s)], axis=0)

    def pair_state(a, b):
        both = dot(a, b, TN)
        return jnp.where(state_low, both[:DH], both[DH:]).astype(BF16)

    positions = (seq * GROUP + iota((GROUP, PAIR), 0)).astype(F32)
    factor = 1.0 / jnp.sqrt(DH * (positions + 1.0))

    loads[0].wait()
    loads[1].wait()
    for p in range(pairs):
        c = slice(p * PAIR, (p + 1) * PAIR)
        state_f[p * DH:(p + 1) * DH, :] = pair_state(k[:, c], v[:, c])

    pl.semaphore_wait(barrier, len(peers))
    for d in range(1, ys):
        to = (y + d) % ys
        send(g_hbm.at[:, cols(to, width)], g.at[rows(y, rows_y)], G, at_y(to))

    def to_columns(src, dst, which):
        for d in range(1, columns):
            o = (column + d) % columns
            send(src.at[rows(o, HALF)], dst.at[rows(column, HALF)], which, at_column(o))
        dst[rows(column, HALF), :] = src[rows(column, HALF), :]

    to_columns(state_f, part_f, P1F)

    r, s = iota((xs * HALF, columns * HALF), 0), iota((xs * HALF, columns * HALF), 1)
    perm_in[...] = jnp.where(
        (r % sub == s % sub)
        & ((r // chunk) == (s // sub) % owners)
        & ((r // sub) % xs == s // (CORES * HALF)),
        1.0, 0.0).astype(BF16)
    r, s = iota((xs * HALF, xs * HALF), 0), iota((xs * HALF, xs * HALF), 1)
    perm_out[...] = jnp.where(
        (r % sub == s % sub)
        & ((s // chunk) == (r // sub) % owners)
        & ((s // sub) % xs == r // HALF),
        1.0, 0.0).astype(BF16)
    r, s = iota((zs * chunk, zs * chunk), 0), iota((zs * chunk, zs * chunk), 1)
    ahead = ((r // sub) % xs - (s // sub) % xs) * zs + r // chunk - s // chunk
    order[...] = jnp.where((r % sub == s % sub) & (ahead * (1 - 2 * (z % 2)) > 0), 1.0, 0.0).astype(BF16)

    causal = iota((2 * GROUP, GROUP), 0) % GROUP >= iota((2 * GROUP, GROUP), 1)
    causal_t = iota((GROUP, 2 * GROUP), 1) % GROUP >= iota((GROUP, 2 * GROUP), 0)

    loads[2].wait()

    def scaled(a):
        return (a.astype(F32) * factor).astype(BF16)

    def inside_forward():
        for p in range(pairs):
            c = slice(p * PAIR, (p + 1) * PAIR)
            scores = jnp.where(causal, dot(split(scaled(q[:, c])), k[:, c], NT), 0.0).astype(BF16)
            attn_l[:, c] = dot(beside(scores), split(v[:, c]))

    def inside_backward():
        for p in range(pairs):
            c = slice(p * PAIR, (p + 1) * PAIR)
            g_two, q_two = split(scaled(g[:, c])), split(q[:, c])
            grad_scores = jnp.where(causal, dot(g_two, v[:, c], NT), 0.0).astype(BF16)
            gq_l[:, c] = dot(beside(grad_scores), split(k[:, c]))
            grad_scores_t = jnp.where(causal_t, dot(v[:, c], g_two, NT), 0.0).astype(BF16)
            gk_l[:, c] = dot(grad_scores_t, q_two)
            plain_t = jnp.where(causal_t, dot(k[:, c], q_two, NT), 0.0).astype(BF16)
            gv_l[:, c] = dot(plain_t, g_two)

    def to_owners(part, chip, which, parity):
        arrived(part.at[pl.ds(0, (columns - 1) * HALF)], which)
        chip[...] = dot(perm_in[...], part[...]).astype(BF16)
        mine = z // 2
        for d in range(owners):
            o = (mine + d) % owners

            def go(o=o):
                send(chip.at[rows(o, chunk)], line.at[rows(z, chunk)], P2, at_z(2 * o + parity))

            if d:
                go()
            else:
                pl.when(z % 2 != parity)(go)

        @pl.when(z % 2 == parity)
        def _():
            line[rows(z, chunk), :] = chip[rows(mine, chunk), :]

    def own(scan, which):
        arrived(line.at[pl.ds(0, (zs - 1) * chunk)], P2)
        line_out[...] = dot(order[...], line[...]).astype(BF16)
        mine = z // 2
        for d in range(1, zs):
            to = (z + d) % zs
            send(line_out.at[rows(to, chunk)], scan.at[rows(mine, chunk)], which, at_z(to))
        scan[rows(mine, chunk), :] = line_out[rows(z, chunk), :]

    def back(scan, part, full, dst, which3, which4, parity):
        @pl.when(z % 2 == parity)
        def _():
            arrived(scan.at[pl.ds(0, (owners - 1) * chunk)], which3)

        @pl.when(z % 2 != parity)
        def _():
            arrived(scan, which3)

        outer = dot(perm_out[...], scan[...])
        for xx in range(xs):
            base = outer[xx * HALF:(xx + 1) * HALF]
            at = xx * CORES * HALF
            plain, more = (at, at + HALF) if parity == 0 else (at + HALF, at)
            full[plain:plain + HALF, :] = base.astype(BF16)
            full[more:more + HALF, :] = (base + part[plain:plain + HALF, :].astype(F32)).astype(BF16)
        to_columns(full, dst, which4)

    inside_forward()
    to_owners(part_f, chip_f, P1F, 0)

    loads[3].wait()
    arrived(g.at[pl.ds(0, (ys - 1) * rows_y)], G)
    for p in range(pairs):
        c = slice(p * PAIR, (p + 1) * PAIR)
        state_r[p * DH:(p + 1) * DH, :] = pair_state(q[:, c], scaled(g[:, c]))
    to_columns(state_r, part_r, P1R)

    pl.when(even)(functools.partial(own, scan_f, P3F))
    to_owners(part_r, chip_r, P1R, 1)
    inside_backward()
    back(scan_f, part_f, full_f, kv, P3F, P4F, 0)
    pl.when(jnp.logical_not(even))(functools.partial(own, scan_r, P3R))

    arrived(kv.at[pl.ds(0, (columns - 1) * HALF)], P4F)
    for p in range(pairs):
        c = slice(p * PAIR, (p + 1) * PAIR)
        state = diagonal(kv[p * DH:(p + 1) * DH, :])
        attn_s[:, c] = (attn_l[:, c] + dot(scaled(q[:, c]), state)).astype(BF16)
    for d in range(1, ys):
        to = (y + d) % ys
        send(attn_s.at[rows(to, rows_y)], attn_r.at[:, cols(y, width)], AT, at_y(to))
    attn_r[:, cols(y, width)] = attn_s[rows(y, rows_y), :]
    for p in range(pairs):
        c = slice(p * PAIR, (p + 1) * PAIR)
        state = diagonal(kv[p * DH:(p + 1) * DH, :])
        gq_s[:, c] = (gq_l[:, c] + dot(scaled(g[:, c]), state, NT)).astype(BF16)
    out_gq = pltpu.make_async_copy(gq_s, gq_o, out_sem.at[0])
    out_gq.start()

    back(scan_r, part_r, full_r, gr, P3R, P4R, 1)
    arrived(attn_r.at[:, pl.ds(0, (ys - 1) * width)], AT)
    out_attn = pltpu.make_async_copy(attn_r, attn_o, out_sem.at[1])
    out_attn.start()

    arrived(gr.at[pl.ds(0, (columns - 1) * HALF)], P4R)
    for p in range(pairs):
        c = slice(p * PAIR, (p + 1) * PAIR)
        state = diagonal(gr[p * DH:(p + 1) * DH, :])
        gk_s[:, c] = (gk_l[:, c] + dot(v[:, c], state, NT)).astype(BF16)
        gv_s[:, c] = (gv_l[:, c] + dot(k[:, c], state)).astype(BF16)
    out_gk = pltpu.make_async_copy(gk_s, gk_o, out_sem.at[2])
    out_gk.start()
    out_gv = pltpu.make_async_copy(gv_s, gv_o, out_sem.at[3])
    out_gv.start()

    sent(g.at[pl.ds(0, (ys - 1) * rows_y)], G)
    for which in (P1F, P1R, P4F, P4R):
        sent(kv.at[pl.ds(0, (columns - 1) * HALF)], which)
    sent(line.at[pl.ds(0, (2 * owners - 1) * chunk)], P2)

    @pl.when(even)
    def _():
        sent(line.at[pl.ds(0, (zs - 1) * chunk)], P3F)

    @pl.when(jnp.logical_not(even))
    def _():
        sent(line.at[pl.ds(0, (zs - 1) * chunk)], P3R)

    sent(attn_r.at[:, pl.ds(0, (ys - 1) * width)], AT)
    for out in (out_gq, out_attn, out_gk, out_gv):
        out.wait()


def shards(xs, zs, ys, query_rot, key_rot, value_rot, grad_out):
    tok, width = query_rot.shape
    columns = xs * CORES
    chunk = xs * (HALF // (zs // 2))
    state = pltpu.VMEM((columns * HALF, PAIR), BF16)
    block = pltpu.VMEM((tok, width), BF16)
    wide = pltpu.VMEM((tok, width), F32)
    half = pltpu.VMEM((xs * HALF, PAIR), BF16)
    line = pltpu.VMEM((zs * chunk, PAIR), BF16)
    any_spec = pl.BlockSpec(memory_space=pl.ANY)
    like = jax.ShapeDtypeStruct((tok, width), BF16)
    return pl.pallas_call(
        functools.partial(kernel, xs, zs, ys),
        out_shape=(jax.ShapeDtypeStruct(grad_out.shape, BF16), like, like, like),
        in_specs=[any_spec] * 4,
        out_specs=(any_spec,) * 4,
        scratch_shapes=[
            block, block, block, block,
            state, state,
            state, state,
            half, half,
            line, line,
            half, half,
            state, state,
            state, state,
            wide, wide, wide, wide,
            block, pltpu.VMEM(grad_out.shape, BF16), block, block, block,
            pltpu.VMEM((xs * HALF, columns * HALF), BF16),
            pltpu.VMEM((xs * HALF, xs * HALF), BF16),
            pltpu.VMEM((zs * chunk, zs * chunk), BF16),
            pltpu.SemaphoreType.DMA((4,)),
            pltpu.SemaphoreType.DMA((4,)),
            pltpu.SemaphoreType.DMA((9,)),
            pltpu.SemaphoreType.DMA((9,)),
        ],
        compiler_params=pltpu.CompilerParams(
            collective_id=0, has_side_effects=True, vmem_limit_bytes=32 * 2**20
        ),
    )(query_rot, key_rot, value_rot, grad_out)


def solution(mesh, xs=XS, zs=ZS):
    in_specs = (P("seq", "head"), P("seq", "head"), P("seq", "head"), P(("seq", "head"), None))
    out_specs = (P(("seq", "head"), None), P("seq", "head"), P("seq", "head"), P("seq", "head"))
    return jax.shard_map(
        functools.partial(shards, xs, zs, mesh.shape["head"]),
        mesh=mesh, in_specs=in_specs, out_specs=out_specs, check_vma=False,
    )
```

time: 551 us -> 53.8 us (0.10)
  waiting for transfers between devices: 377 us -> 0 us
  other arithmetic: 130 us -> 0 us
  Pallas kernels: 0 us -> 46.8 us
  between operations: 14.2 us -> 0.65 us
  starting transfers between devices: 9.05 us -> 0 us
    all_gather x2 -> x0, waiting for transfers between devices: 368 us -> none  [prefix(): gathered = lax.all_gather(part, axis)]
    add x127 -> x0, other arithmetic: 129 us -> none  [add_states(): return earlier + later]
    pallas_call x0 -> x1, Pallas kernels: none -> 46.8 us  [shards(): pl.pallas_call(functools.partial(kernel, xs, zs, ys), out_shape=(jax.Shap...]
    all_to_all x2 -> x0, starting transfers between devices: 9.01 us -> none  [the longest x1 5.01 us: shards(): lax.all_to_all(grad_out, 'head', split_axis=1, concat_axis=0, tiled=True)]
    all_to_all x2 -> x0, waiting for transfers between devices: 8.57 us -> none  [the longest x1 4.79 us: shards(): lax.all_to_all(attn_local, 'head', split_axis=0, concat_axis=1, tiled=True)]
  transfers between devices with their start and end apart: 4 -> 0, of which waited for: 4 -> 0; matrix products, arithmetic and copies ran while one was open for 2% -> 0% of each run, Pallas kernels for 0% -> 0%
where the time goes in v1:
time: 53.8 us; the launch traced here: 53.7 us
  Pallas kernels  46.8 us (87%)
  local copies, waits for them, and re-layouts  6.23 us (12%)
  between operations  0.65 us (1%)
    pallas_call x1, Pallas kernels, shards(): pl.pallas_call(functools.partial(kernel, xs, zs, ys), out_shape=(jax.Shap...  46.8 us
    unnamed x12, local copies, waits for them, and re-layouts  6.23 us

profile of v1, /device:TPU:1, one launch (start us, length us, event | category | flops | bytes accessed | tf_op | source)
XLA Modules:
  0.0 53.7 jit_solution(3709054460011511684)
XLA Ops:
  0.6 0.0 copy-start
  0.6 0.9 %copy-done = bf16[128,512]{1,0:T(8,128)(2,1)S(1)} copy-done((bf16[128,512]{1,0:T(8,128)(2,1)S(1)}, bf16[128,512]{1,0:T(8,128)(2,1)}, u32[]{:S(2)}) %copy-start) | copy-done | bytes 131096
  1.5 0.0 copy-start.1
  1.5 0.9 %copy-done.1 = bf16[128,512]{1,0:T(8,128)(2,1)S(1)} copy-done((bf16[128,512]{1,0:T(8,128)(2,1)S(1)}, bf16[128,512]{1,0:T(8,128)(2,1)}, u32[]{:S(2)}) %copy-start.1) | copy-done | bytes 131096
  2.4 0.0 copy-start.2
  2.4 0.9 %copy-done.2 = bf16[128,512]{1,0:T(8,128)(2,1)S(1)} copy-done((bf16[128,512]{1,0:T(8,128)(2,1)S(1)}, bf16[128,512]{1,0:T(8,128)(2,1)}, u32[]{:S(2)}) %copy-start.2) | copy-done | bytes 131096
  3.3 0.0 copy-start.3
  3.3 0.9 %copy-done.3 = bf16[32,2048]{1,0:T(8,128)(2,1)S(1)} copy-done((bf16[32,2048]{1,0:T(8,128)(2,1)S(1)}, bf16[32,2048]{1,0:T(8,128)(2,1)}, u32[]{:S(2)}) %copy-start.3) | copy-done | bytes 131096
  4.3 46.8 %shard_map.75 = (bf16[32,2048]{1,0:T(8,128)(2,1)S(1)}, bf16[128,512]{1,0:T(8,128)(2,1)S(1)}, bf16[128,512]{1,0:T(8,128)(2,1)S(1)}, bf16[128,512]{1,0:T(8,128)(2,1)S(1)}) custom-call(bf16[128,512]{1,0:T(8,128)(2,1)S(1)} %copy-done, bf16[128,512]{1,0:T(8,128)(2,1)S(1)} %copy-done.1, bf16[128,512]{1,0:T(8,128)(2,1)S(1)} %copy-done.2, bf16[32,2048]{1,0:T(8,128)(2,1)S(1)} %copy-done.3), custom_call_target="tpu_custom_call" | custom-call | tf_op jit(solution)/shard_map/pallas_call | solution.py:321
  51.0 0.7 %copy.12 = bf16[32,2048]{1,0:T(8,128)(2,1)} copy(bf16[32,2048]{1,0:T(8,128)(2,1)S(1)} %get-tuple-element.8) | data formatting | bytes 262144
  51.7 0.7 %copy.13 = bf16[128,512]{1,0:T(8,128)(2,1)} copy(bf16[128,512]{1,0:T(8,128)(2,1)S(1)} %get-tuple-element.9) | data formatting | bytes 262144
  52.3 0.7 %copy.14 = bf16[128,512]{1,0:T(8,128)(2,1)} copy(bf16[128,512]{1,0:T(8,128)(2,1)S(1)} %get-tuple-element.10) | data formatting | bytes 262144
  53.0 0.7 %copy.15 = bf16[128,512]{1,0:T(8,128)(2,1)} copy(bf16[128,512]{1,0:T(8,128)(2,1)S(1)} %get-tuple-element.11) | data formatting | bytes 262144
Async XLA Ops:
  0.6 0.9 %copy-start = (bf16[128,512]{1,0:T(8,128)(2,1)S(1)}, bf16[128,512]{1,0:T(8,128)(2,1)}, u32[]{:S(2)}) copy-start(bf16[128,512]{1,0:T(8,128)(2,1)} %q_hbm.1) | copy-start | bytes 393220
  1.5 0.9 %copy-start.1 = (bf16[128,512]{1,0:T(8,128)(2,1)S(1)}, bf16[128,512]{1,0:T(8,128)(2,1)}, u32[]{:S(2)}) copy-start(bf16[128,512]{1,0:T(8,128)(2,1)} %k_hbm.1) | copy-start | bytes 393220
  2.4 0.9 %copy-start.2 = (bf16[128,512]{1,0:T(8,128)(2,1)S(1)}, bf16[128,512]{1,0:T(8,128)(2,1)}, u32[]{:S(2)}) copy-start(bf16[128,512]{1,0:T(8,128)(2,1)} %v_hbm.1) | copy-start | bytes 393220
  3.3 0.9 %copy-start.3 = (bf16[32,2048]{1,0:T(8,128)(2,1)S(1)}, bf16[32,2048]{1,0:T(8,128)(2,1)}, u32[]{:S(2)}) copy-start(bf16[32,2048]{1,0:T(8,128)(2,1)} %g_hbm.1) | copy-start | bytes 393220

commit v2 on v1

v2 whole, which is shorter than its diff:
```python
import functools

import jax
import jax.numpy as jnp
from jax import lax
from jax.experimental import pallas as pl
from jax.experimental.pallas import tpu as pltpu
from jax.sharding import PartitionSpec as P

DH = 64
GROUP = 128
XS = 4
ZS = 16
CORES = 2
PAIR = 2 * DH
HALF = DH // CORES
FORWARD_AT = (0, 2, 4, 15)
BACKWARD_AT = (1, 3, 5, 14)
BACK_ORDER = (0, 1, 2, 3, 4, 15, 5, 14, 6, 13, 7, 12, 8, 11, 9, 10)
MESH = pl.DeviceIdType.MESH
F32 = jnp.float32
BF16 = jnp.bfloat16

NN = (((1,), (0,)), ((), ()))
NT = (((1,), (1,)), ((), ()))
TN = (((0,), (0,)), ((), ()))
G, CF, CR, OUT, TOT, BF, BR, AT = range(8)


def dot(a, b, dims=NN):
    return lax.dot_general(a, b, dims, preferred_element_type=F32)


def iota(shape, dim):
    return lax.broadcasted_iota(jnp.int32, shape, dim)


def kernel(
    xs, zs, ys, forward_at, backward_at, back_order,
    q_hbm, k_hbm, v_hbm, g_hbm,
    attn_o, gq_o, gk_o, gv_o,
    q, k, v, g,
    own_f, own_r, sib_f, sib_r,
    chip_f, chip_r,
    line, part, line_out,
    totals,
    scan_f, scan_r,
    attn_l, gq_l, gk_l, gv_l,
    attn_s, attn_r, gq_s, gk_s, gv_s,
    in_sem, out_sem, send_sem, recv_sem,
):
    width = q.shape[1]
    pairs = width // PAIR
    half = pairs * HALF
    chunk = half // len(forward_at)
    rows_y = GROUP // ys

    seq = lax.axis_index("seq")
    y = lax.axis_index("head")
    x = seq // (zs * CORES)
    z = (seq // CORES) % zs
    core = seq % CORES

    def device(xx, zz, cc):
        return ((xx * zs + zz) * CORES + cc, y)

    def among(zz, places):
        found = zz == places[0]
        for place in places[1:]:
            found = jnp.logical_or(found, zz == place)
        return found

    def aligned(i, n):
        return pl.ds(pl.multiple_of(i * n, n), n)

    def send(src, dst, which, to):
        pltpu.make_async_remote_copy(
            src_ref=src, dst_ref=dst, send_sem=send_sem.at[which], recv_sem=recv_sem.at[which],
            device_id=to, device_id_type=MESH,
        ).start()

    def arrived(ref, which):
        pltpu.make_async_copy(ref, ref, recv_sem.at[which]).wait()

    def sent(ref, which):
        pltpu.make_async_copy(ref, ref, send_sem.at[which]).wait()

    barrier = pltpu.get_barrier_semaphore()
    both = forward_at + backward_at
    owner = among(z, both)
    sibling = device(x, z, 1 - core)

    def greet(to):
        pl.semaphore_signal(barrier, inc=1, device_id=to, device_id_type=MESH)

    for zz in range(zs):
        for cc in range(CORES):
            near = jnp.logical_and(z == zz, core == cc)
            if zz in both:
                meet = jnp.logical_not(near)
            else:
                meet = jnp.logical_and(jnp.logical_or(owner, z == zz), jnp.logical_not(near))
            pl.when(meet)(functools.partial(greet, device(x, zz, cc)))
    for d in range(1, ys):
        greet((seq, (y + d) % ys))
    for d in range(1, xs):
        greet(device((x + d) % xs, z, core))
    greeted = ys - 1 + xs - 1 + jnp.where(owner, CORES * zs - 1, CORES * len(both) + 1)

    loads = [
        pltpu.make_async_copy(src, dst, in_sem.at[i])
        for i, (src, dst) in enumerate(
            (
                (k_hbm, k), (v_hbm, v), (q_hbm, q),
                (g_hbm.at[:, aligned(y, width)], g.at[aligned(y, rows_y)]),
            )
        )
    ]
    for load in loads:
        load.start()

    lane_low = iota((GROUP, PAIR), 1) < DH
    state_low = iota((DH, PAIR), 1) < DH

    def split(a):
        return jnp.concatenate([jnp.where(lane_low, a, 0), jnp.where(lane_low, 0, a)], axis=0)

    def beside(a):
        return jnp.concatenate([a[:GROUP], a[GROUP:]], axis=1)

    def diagonal(s):
        return jnp.concatenate([jnp.where(state_low, s, 0), jnp.where(state_low, 0, s)], axis=0)

    def columns(p):
        return slice(p * PAIR, (p + 1) * PAIR)

    def at(h, p):
        return slice(h * half + p * HALF, h * half + (p + 1) * HALF)

    def pair_state(own, p, a, b):
        product = dot(a, b, TN)
        state = jnp.where(state_low, product[:DH], product[DH:])
        for h in range(CORES):
            own[at(h, p), :] = state[h * HALF:(h + 1) * HALF]

    positions = (seq * GROUP + iota((GROUP, PAIR), 0)).astype(F32)
    factor = 1.0 / jnp.sqrt(DH * (positions + 1.0))

    def scaled(a):
        return (a.astype(F32) * factor).astype(BF16)

    def to_owners(own, sib, chip, which, places):
        arrived(sib, which)
        mine = aligned(core, half)
        chip[...] = (own[mine, :] + sib[mine, :]).astype(BF16)
        for i, place in enumerate(places):
            piece = chip.at[pl.ds(i * chunk, chunk)]

            @pl.when(z != place)
            def _(piece=piece, place=place):
                send(piece, line.at[aligned(z, chunk)], OUT, device(x, place, core))

            @pl.when(z == place)
            def _(i=i, place=place):
                line[place * chunk:(place + 1) * chunk, :] = chip[i * chunk:(i + 1) * chunk, :]

    def own_chunk(scan, which, i, place, backward):
        arrived(line.at[pl.ds(0, (zs - 1) * chunk)], OUT)
        total = None
        for step in range(zs):
            zz = zs - 1 - step if backward else step
            piece = line[zz * chunk:(zz + 1) * chunk, :].astype(F32)
            part[zz * chunk:(zz + 1) * chunk, :] = jnp.zeros_like(piece) if total is None else total
            total = piece if total is None else total + piece
        totals[aligned(x, chunk), :] = total
        for d in range(1, xs):
            send(totals.at[aligned(x, chunk)], totals.at[aligned(x, chunk)], TOT, device((x + d) % xs, place, core))
        arrived(totals.at[pl.ds(0, (xs - 1) * chunk)], TOT)
        base = jnp.zeros_like(total)
        for xx in range(xs):
            counts = xx > x if backward else xx < x
            base = base + jnp.where(counts, totals[xx * chunk:(xx + 1) * chunk, :], 0.0)
        for zz in range(zs):
            line_out[zz * chunk:(zz + 1) * chunk, :] = (part[zz * chunk:(zz + 1) * chunk, :] + base).astype(BF16)
        home = pl.ds(pl.multiple_of(core * half + i * chunk, chunk), chunk)
        for zz in back_order:
            piece = line_out.at[pl.ds(zz * chunk, chunk)]
            if zz == place:
                send(piece, scan.at[home], which, sibling)
                scan[home, :] = line_out[zz * chunk:(zz + 1) * chunk, :]
            else:
                for cc in range(CORES):
                    send(piece, scan.at[home], which, device(x, zz, cc))

    def own_one(scan, which, places, backward):
        for i, place in enumerate(places):
            pl.when(z == place)(functools.partial(own_chunk, scan, which, i, place, backward))

    def came_back(scan, which, places):
        mine = among(z, places)

        @pl.when(mine)
        def _():
            arrived(scan.at[pl.ds(0, CORES * half - chunk)], which)

        @pl.when(jnp.logical_not(mine))
        def _():
            arrived(scan, which)

    def state_of(scan, sib, weight, p):
        rows = [scan[at(h, p), :].astype(F32) + weight * sib[at(h, p), :] for h in range(CORES)]
        return diagonal(jnp.concatenate(rows, axis=0)).astype(BF16)

    loads[0].wait()
    loads[1].wait()
    for p in range(pairs):
        pair_state(own_f, p, k[:, columns(p)], v[:, columns(p)])
    pl.semaphore_wait(barrier, greeted)
    for d in range(1, ys):
        to = (y + d) % ys
        send(g_hbm.at[:, aligned(to, width)], g.at[aligned(y, rows_y)], G, (seq, to))
    send(own_f, sib_f, CF, sibling)

    causal = iota((2 * GROUP, GROUP), 0) % GROUP >= iota((2 * GROUP, GROUP), 1)
    causal_t = iota((GROUP, 2 * GROUP), 1) % GROUP >= iota((GROUP, 2 * GROUP), 0)
    to_owners(own_f, sib_f, chip_f, CF, forward_at)

    loads[2].wait()
    for p in range(pairs):
        c = columns(p)
        scores = jnp.where(causal, dot(split(scaled(q[:, c])), k[:, c], NT), 0.0).astype(BF16)
        attn_l[:, c] = dot(beside(scores), split(v[:, c]))

    loads[3].wait()
    arrived(g.at[pl.ds(0, (ys - 1) * rows_y)], G)
    for p in range(pairs):
        pair_state(own_r, p, q[:, columns(p)], scaled(g[:, columns(p)]))
    send(own_r, sib_r, CR, sibling)
    to_owners(own_r, sib_r, chip_r, CR, backward_at)

    for p in range(pairs):
        c = columns(p)
        g_two, q_two = split(scaled(g[:, c])), split(q[:, c])
        grad_scores = jnp.where(causal, dot(g_two, v[:, c], NT), 0.0).astype(BF16)
        gq_l[:, c] = dot(beside(grad_scores), split(k[:, c]))
        grad_scores_t = jnp.where(causal_t, dot(v[:, c], g_two, NT), 0.0).astype(BF16)
        gk_l[:, c] = dot(grad_scores_t, q_two)
        plain_t = jnp.where(causal_t, dot(k[:, c], q_two, NT), 0.0).astype(BF16)
        gv_l[:, c] = dot(plain_t, g_two)

    own_one(scan_f, BF, forward_at, False)
    own_one(scan_r, BR, backward_at, True)

    after = core.astype(F32)
    came_back(scan_f, BF, forward_at)
    for p in range(pairs):
        c = columns(p)
        state = state_of(scan_f, sib_f, after, p)
        attn_s[:, c] = (attn_l[:, c] + dot(scaled(q[:, c]), state)).astype(BF16)
    for d in range(1, ys):
        to = (y + d) % ys
        send(attn_s.at[aligned(to, rows_y)], attn_r.at[:, aligned(y, width)], AT, (seq, to))
    attn_r[:, aligned(y, width)] = attn_s[aligned(y, rows_y), :]
    for p in range(pairs):
        c = columns(p)
        state = state_of(scan_f, sib_f, after, p)
        gq_s[:, c] = (gq_l[:, c] + dot(scaled(g[:, c]), state, NT)).astype(BF16)
    out_gq = pltpu.make_async_copy(gq_s, gq_o, out_sem.at[0])
    out_gq.start()

    came_back(scan_r, BR, backward_at)
    for p in range(pairs):
        c = columns(p)
        state = state_of(scan_r, sib_r, 1.0 - after, p)
        gk_s[:, c] = (gk_l[:, c] + dot(v[:, c], state, NT)).astype(BF16)
        gv_s[:, c] = (gv_l[:, c] + dot(k[:, c], state)).astype(BF16)
    out_gk = pltpu.make_async_copy(gk_s, gk_o, out_sem.at[1])
    out_gk.start()
    out_gv = pltpu.make_async_copy(gv_s, gv_o, out_sem.at[2])
    out_gv.start()

    arrived(attn_r.at[:, pl.ds(0, (ys - 1) * width)], AT)
    out_attn = pltpu.make_async_copy(attn_r, attn_o, out_sem.at[3])
    out_attn.start()

    sent(g.at[pl.ds(0, (ys - 1) * rows_y)], G)
    sent(own_f, CF)
    sent(own_r, CR)
    sent(attn_r.at[:, pl.ds(0, (ys - 1) * width)], AT)

    @pl.when(jnp.logical_not(owner))
    def _():
        sent(chip_f, OUT)
        sent(chip_r, OUT)

    @pl.when(owner)
    def _():
        sent(chip_f, OUT)
        sent(chip_r.at[pl.ds(0, half - chunk)], OUT)
        sent(totals.at[pl.ds(0, (xs - 1) * chunk)], TOT)

    for places, which in ((forward_at, BF), (backward_at, BR)):

        @pl.when(among(z, places))
        def _(which=which):
            sent(line_out, which)
            sent(line_out.at[pl.ds(0, (zs - 1) * chunk)], which)

    for out in (out_gq, out_gk, out_gv, out_attn):
        out.wait()


def shards(xs, zs, ys, forward_at, backward_at, back_order, query_rot, key_rot, value_rot, grad_out):
    tok, width = query_rot.shape
    half = width // PAIR * HALF
    chunk = half // len(forward_at)
    block = pltpu.VMEM((tok, width), BF16)
    wide = pltpu.VMEM((tok, width), F32)
    state = pltpu.VMEM((CORES * half, PAIR), F32)
    chip = pltpu.VMEM((half, PAIR), BF16)
    line = pltpu.VMEM((zs * chunk, PAIR), BF16)
    scan = pltpu.VMEM((CORES * half, PAIR), BF16)
    like = jax.ShapeDtypeStruct((tok, width), BF16)
    return pl.pallas_call(
        functools.partial(kernel, xs, zs, ys, forward_at, backward_at, back_order),
        out_shape=(jax.ShapeDtypeStruct(grad_out.shape, BF16), like, like, like),
        in_specs=[pl.BlockSpec(memory_space=pltpu.HBM)] * 4,
        out_specs=(pl.BlockSpec(memory_space=pl.ANY),) * 4,
        scratch_shapes=[
            block, block, block, block,
            state, state, state, state,
            chip, chip,
            line, pltpu.VMEM((zs * chunk, PAIR), F32), line,
            pltpu.VMEM((xs * chunk, PAIR), F32),
            scan, scan,
            wide, wide, wide, wide,
            block, pltpu.VMEM(grad_out.shape, BF16), block, block, block,
            pltpu.SemaphoreType.DMA((4,)),
            pltpu.SemaphoreType.DMA((4,)),
            pltpu.SemaphoreType.DMA((8,)),
            pltpu.SemaphoreType.DMA((8,)),
        ],
        compiler_params=pltpu.CompilerParams(
            collective_id=0, has_side_effects=True, vmem_limit_bytes=63 * 2**20
        ),
    )(query_rot, key_rot, value_rot, grad_out)


def solution(mesh, xs=XS, zs=ZS, forward_at=FORWARD_AT, backward_at=BACKWARD_AT, back_order=BACK_ORDER):
    in_specs = (P("seq", "head"), P("seq", "head"), P("seq", "head"), P(("seq", "head"), None))
    out_specs = (P(("seq", "head"), None), P("seq", "head"), P("seq", "head"), P("seq", "head"))
    return jax.shard_map(
        functools.partial(shards, xs, zs, mesh.shape["head"], forward_at, backward_at, back_order),
        mesh=mesh, in_specs=in_specs, out_specs=out_specs, check_vma=False,
    )
```

time: 53.8 us -> 45.2 us (0.84)
  Pallas kernels: 46.8 us -> 40.2 us
  local copies, waits for them, and re-layouts: 6.23 us -> 4.16 us
    pallas_call x1, Pallas kernels: 46.8 us -> 40.2 us  [shards(): pl.pallas_call(functools.partial(kernel, xs, zs, ys, forward_at, backward...]
    unnamed x12 -> x10, local copies, waits for them, and re-layouts: 6.23 us -> 4.16 us
where the time goes in v2:
time: 45.2 us; the launch traced here: 45 us
  Pallas kernels  40.2 us (89%)
  local copies, waits for them, and re-layouts  4.16 us (9%)
  between operations  0.65 us (1%)
    pallas_call x1, Pallas kernels, shards(): pl.pallas_call(functools.partial(kernel, xs, zs, ys, forward_at, backward...  40.2 us
    unnamed x10, local copies, waits for them, and re-layouts  4.16 us

profile of v2, /device:TPU:1, one launch (start us, length us, event | category | flops | bytes accessed | tf_op | source)
XLA Modules:
  0.0 45.0 jit_solution(8397640243167751470)
XLA Ops:
  0.6 40.2 %shard_map.75 = (bf16[32,2048]{1,0:T(8,128)(2,1)}, bf16[128,512]{1,0:T(8,128)(2,1)}, bf16[128,512]{1,0:T(8,128)(2,1)}, bf16[128,512]{1,0:T(8,128)(2,1)}) custom-call(bf16[128,512]{1,0:T(8,128)(2,1)} %q_hbm.1, bf16[128,512]{1,0:T(8,128)(2,1)} %k_hbm.1, bf16[128,512]{1,0:T(8,128)(2,1)} %v_hbm.1, bf16[32,2048]{1,0:T(8,128)(2,1)} %g_hbm.1), custom_call_target="tpu_custom_call" | custom-call | tf_op jit(solution)/shard_map/pallas_call | solution.py:324
  40.8 0.0 copy-start.2
  40.8 1.6 %copy.12 = bf16[32,2048]{1,0:T(8,128)(2,1)} copy(bf16[32,2048]{1,0:T(8,128)(2,1)} %get-tuple-element.8) | data formatting | bytes 262144
  42.4 0.0 copy-done.2
  42.4 0.0 copy-start.1
  42.4 0.7 %copy.13 = bf16[128,512]{1,0:T(8,128)(2,1)} copy(bf16[128,512]{1,0:T(8,128)(2,1)S(1)} %copy-done.2) | data formatting | bytes 262144
  43.1 0.3 copy-done.1
  43.4 0.0 copy-start
  43.4 0.7 %copy.14 = bf16[128,512]{1,0:T(8,128)(2,1)} copy(bf16[128,512]{1,0:T(8,128)(2,1)S(1)} %copy-done.1) | data formatting | bytes 262144
  44.0 0.3 copy-done
  44.3 0.7 %copy.15 = bf16[128,512]{1,0:T(8,128)(2,1)} copy(bf16[128,512]{1,0:T(8,128)(2,1)S(1)} %copy-done) | data formatting | bytes 262144
Async XLA Ops:
  40.8 1.6 %copy-start.2 = (bf16[128,512]{1,0:T(8,128)(2,1)S(1)}, bf16[128,512]{1,0:T(8,128)(2,1)}, u32[]{:S(2)}) copy-start(bf16[128,512]{1,0:T(8,128)(2,1)} %get-tuple-element.9) | copy-start | bytes 393220
  42.4 1.0 %copy-start.1 = (bf16[128,512]{1,0:T(8,128)(2,1)S(1)}, bf16[128,512]{1,0:T(8,128)(2,1)}, u32[]{:S(2)}) copy-start(bf16[128,512]{1,0:T(8,128)(2,1)} %get-tuple-element.10) | copy-start | bytes 393220
  43.4 1.0 %copy-start = (bf16[128,512]{1,0:T(8,128)(2,1)S(1)}, bf16[128,512]{1,0:T(8,128)(2,1)}, u32[]{:S(2)}) copy-start(bf16[128,512]{1,0:T(8,128)(2,1)} %get-tuple-element.11) | copy-start | bytes 393220

commit v3 on v2

--- a/solution.py
+++ b/solution.py
@@ -14,9 +14,9 @@
 CORES = 2
 PAIR = 2 * DH
 HALF = DH // CORES
-FORWARD_AT = (0, 2, 4, 15)
-BACKWARD_AT = (1, 3, 5, 14)
-BACK_ORDER = (0, 1, 2, 3, 4, 15, 5, 14, 6, 13, 7, 12, 8, 11, 9, 10)
+FORWARD_AT = (12, 14, 0, 2)
+BACKWARD_AT = (13, 15, 1, 3)
+BACK_ORDER = (0, 1, 2, 15, 3, 14, 4, 13, 5, 12, 6, 11, 7, 10, 8, 9)
 MESH = pl.DeviceIdType.MESH
 F32 = jnp.float32
 BF16 = jnp.bfloat16
@@ -38,16 +38,16 @@
 def kernel(
     xs, zs, ys, forward_at, backward_at, back_order,
     q_hbm, k_hbm, v_hbm, g_hbm,
-    attn_o, gq_o, gk_o, gv_o,
-    q, k, v, g,
+    attn_r, gq_s, gk_s, gv_s,
+    q, k, v, g_in, g,
     own_f, own_r, sib_f, sib_r,
     chip_f, chip_r,
     line, part, line_out,
     totals,
     scan_f, scan_r,
     attn_l, gq_l, gk_l, gv_l,
-    attn_s, attn_r, gq_s, gk_s, gv_s,
-    in_sem, out_sem, send_sem, recv_sem,
+    attn_s,
+    in_sem, send_sem, recv_sem,
 ):
     width = q.shape[1]
     pairs = width // PAIR
@@ -93,26 +93,22 @@
     def greet(to):
         pl.semaphore_signal(barrier, inc=1, device_id=to, device_id_type=MESH)
 
-    for zz in range(zs):
-        for cc in range(CORES):
-            near = jnp.logical_and(z == zz, core == cc)
-            if zz in both:
-                meet = jnp.logical_not(near)
-            else:
-                meet = jnp.logical_and(jnp.logical_or(owner, z == zz), jnp.logical_not(near))
-            pl.when(meet)(functools.partial(greet, device(x, zz, cc)))
     for d in range(1, ys):
         greet((seq, (y + d) % ys))
     for d in range(1, xs):
         greet(device((x + d) % xs, z, core))
-    greeted = ys - 1 + xs - 1 + jnp.where(owner, CORES * zs - 1, CORES * len(both) + 1)
+    greet(sibling)
+    for zz in range(zs):
+        for cc in range(CORES):
+            meet = jnp.logical_and(True if zz in both else owner, z != zz)
+            pl.when(meet)(functools.partial(greet, device(x, zz, cc)))
+    greeted = ys - 1 + xs - 1 + 1 + CORES * jnp.where(owner, zs - 1, len(both))
 
     loads = [
         pltpu.make_async_copy(src, dst, in_sem.at[i])
         for i, (src, dst) in enumerate(
             (
-                (k_hbm, k), (v_hbm, v), (q_hbm, q),
-                (g_hbm.at[:, aligned(y, width)], g.at[aligned(y, rows_y)]),
+                (k_hbm, k), (v_hbm, v), (g_hbm, g_in), (q_hbm, q),
             )
         )
     ]
@@ -173,9 +169,19 @@
             part[zz * chunk:(zz + 1) * chunk, :] = jnp.zeros_like(piece) if total is None else total
             total = piece if total is None else total + piece
         totals[aligned(x, chunk), :] = total
-        for d in range(1, xs):
-            send(totals.at[aligned(x, chunk)], totals.at[aligned(x, chunk)], TOT, device((x + d) % xs, place, core))
-        arrived(totals.at[pl.ds(0, (xs - 1) * chunk)], TOT)
+        for xx in range(xs):
+            def pass_on(xx=xx):
+                send(totals.at[aligned(x, chunk)], totals.at[aligned(x, chunk)], TOT, device(xx, place, core))
+
+            pl.when(xx < x if backward else xx > x)(pass_on)
+        waits = (lambda xx: xs - 1 - xx) if backward else (lambda xx: xx)
+        for xx in range(xs):
+            if waits(xx):
+
+                @pl.when(x == xx)
+                def _(n=waits(xx)):
+                    arrived(totals.at[pl.ds(0, n * chunk)], TOT)
+
         base = jnp.zeros_like(total)
         for xx in range(xs):
             counts = xx > x if backward else xx < x
@@ -215,23 +221,24 @@
     loads[1].wait()
     for p in range(pairs):
         pair_state(own_f, p, k[:, columns(p)], v[:, columns(p)])
+    loads[2].wait()
     pl.semaphore_wait(barrier, greeted)
     for d in range(1, ys):
         to = (y + d) % ys
-        send(g_hbm.at[:, aligned(to, width)], g.at[aligned(y, rows_y)], G, (seq, to))
+        send(g_in.at[:, aligned(to, width)], g.at[aligned(y, rows_y)], G, (seq, to))
     send(own_f, sib_f, CF, sibling)
+    g[aligned(y, rows_y), :] = g_in[:, aligned(y, width)]
 
     causal = iota((2 * GROUP, GROUP), 0) % GROUP >= iota((2 * GROUP, GROUP), 1)
     causal_t = iota((GROUP, 2 * GROUP), 1) % GROUP >= iota((GROUP, 2 * GROUP), 0)
     to_owners(own_f, sib_f, chip_f, CF, forward_at)
 
-    loads[2].wait()
+    loads[3].wait()
     for p in range(pairs):
         c = columns(p)
         scores = jnp.where(causal, dot(split(scaled(q[:, c])), k[:, c], NT), 0.0).astype(BF16)
         attn_l[:, c] = dot(beside(scores), split(v[:, c]))
 
-    loads[3].wait()
     arrived(g.at[pl.ds(0, (ys - 1) * rows_y)], G)
     for p in range(pairs):
         pair_state(own_r, p, q[:, columns(p)], scaled(g[:, columns(p)]))
@@ -265,8 +272,6 @@
         c = columns(p)
         state = state_of(scan_f, sib_f, after, p)
         gq_s[:, c] = (gq_l[:, c] + dot(scaled(g[:, c]), state, NT)).astype(BF16)
-    out_gq = pltpu.make_async_copy(gq_s, gq_o, out_sem.at[0])
-    out_gq.start()
 
     came_back(scan_r, BR, backward_at)
     for p in range(pairs):
@@ -274,14 +279,8 @@
         state = state_of(scan_r, sib_r, 1.0 - after, p)
         gk_s[:, c] = (gk_l[:, c] + dot(v[:, c], state, NT)).astype(BF16)
         gv_s[:, c] = (gv_l[:, c] + dot(k[:, c], state)).astype(BF16)
-    out_gk = pltpu.make_async_copy(gk_s, gk_o, out_sem.at[1])
-    out_gk.start()
-    out_gv = pltpu.make_async_copy(gv_s, gv_o, out_sem.at[2])
-    out_gv.start()
 
     arrived(attn_r.at[:, pl.ds(0, (ys - 1) * width)], AT)
-    out_attn = pltpu.make_async_copy(attn_r, attn_o, out_sem.at[3])
-    out_attn.start()
 
     sent(g.at[pl.ds(0, (ys - 1) * rows_y)], G)
     sent(own_f, CF)
@@ -297,7 +296,6 @@
     def _():
         sent(chip_f, OUT)
         sent(chip_r.at[pl.ds(0, half - chunk)], OUT)
-        sent(totals.at[pl.ds(0, (xs - 1) * chunk)], TOT)
 
     for places, which in ((forward_at, BF), (backward_at, BR)):
 
@@ -305,9 +303,18 @@
         def _(which=which):
             sent(line_out, which)
             sent(line_out.at[pl.ds(0, (zs - 1) * chunk)], which)
-
-    for out in (out_gq, out_gk, out_gv, out_attn):
-        out.wait()
+            for xx in range(xs):
+                n = xx if which == BR else xs - 1 - xx
+                if n:
+                    pl.when(x == xx)(functools.partial(sent, totals.at[pl.ds(0, n * chunk)], TOT))
+
+
+def write_out(*refs):
+    copies = [pltpu.make_async_copy(refs[i], refs[4 + i], refs[8].at[i]) for i in range(4)]
+    for copy in copies:
+        copy.start()
+    for copy in copies:
+        copy.wait()
 
 
 def shards(xs, zs, ys, forward_at, backward_at, back_order, query_rot, key_rot, value_rot, grad_out):
@@ -320,30 +327,36 @@
     chip = pltpu.VMEM((half, PAIR), BF16)
     line = pltpu.VMEM((zs * chunk, PAIR), BF16)
     scan = pltpu.VMEM((CORES * half, PAIR), BF16)
-    like = jax.ShapeDtypeStruct((tok, width), BF16)
-    return pl.pallas_call(
+    operands = [pltpu.with_memory_space_constraint(a, pltpu.HBM) for a in (query_rot, key_rot, value_rot, grad_out)]
+    results = pl.pallas_call(
         functools.partial(kernel, xs, zs, ys, forward_at, backward_at, back_order),
-        out_shape=(jax.ShapeDtypeStruct(grad_out.shape, BF16), like, like, like),
+        out_shape=(pltpu.VMEM(grad_out.shape, BF16), block, block, block),
         in_specs=[pl.BlockSpec(memory_space=pltpu.HBM)] * 4,
-        out_specs=(pl.BlockSpec(memory_space=pl.ANY),) * 4,
+        out_specs=(pl.BlockSpec(memory_space=pltpu.VMEM),) * 4,
         scratch_shapes=[
-            block, block, block, block,
+            block, block, block, pltpu.VMEM(grad_out.shape, BF16), block,
             state, state, state, state,
             chip, chip,
             line, pltpu.VMEM((zs * chunk, PAIR), F32), line,
             pltpu.VMEM((xs * chunk, PAIR), F32),
             scan, scan,
             wide, wide, wide, wide,
-            block, pltpu.VMEM(grad_out.shape, BF16), block, block, block,
-            pltpu.SemaphoreType.DMA((4,)),
+            block,
             pltpu.SemaphoreType.DMA((4,)),
             pltpu.SemaphoreType.DMA((8,)),
             pltpu.SemaphoreType.DMA((8,)),
         ],
         compiler_params=pltpu.CompilerParams(
-            collective_id=0, has_side_effects=True, vmem_limit_bytes=63 * 2**20
+            collective_id=0, has_side_effects=True, vmem_limit_bytes=32 * 2**20
         ),
-    )(query_rot, key_rot, value_rot, grad_out)
+    )(*operands)
+    return pl.pallas_call(
+        write_out,
+        out_shape=tuple(jax.ShapeDtypeStruct(a.shape, a.dtype) for a in results),
+        in_specs=[pl.BlockSpec(memory_space=pltpu.VMEM)] * 4,
+        out_specs=(pl.BlockSpec(memory_space=pltpu.HBM),) * 4,
+        scratch_shapes=[pltpu.SemaphoreType.DMA((4,))],
+    )(*[pltpu.with_memory_space_constraint(a, pltpu.VMEM) for a in results])
 
 
 def solution(mesh, xs=XS, zs=ZS, forward_at=FORWARD_AT, backward_at=BACKWARD_AT, back_order=BACK_ORDER):

time: 45.2 us -> 39.9 us (0.88)
  local copies, waits for them, and re-layouts: 4.16 us -> 0 us
  Pallas kernels: 40.2 us -> 39.1 us
    unnamed x10 -> x0, local copies, waits for them, and re-layouts: 4.16 us -> none
    pallas_call x1, Pallas kernels: 40.2 us -> 38.3 us  [shards(): pl.pallas_call(functools.partial(kernel, xs, zs, ys, forward_at, backward...]
    pallas_call x0 -> x1, Pallas kernels: none -> 0.82 us  [shards(): pl.pallas_call(write_out, out_shape=tuple((jax.ShapeDtypeStruct(a.shape,...]
where the time goes in v3:
time: 39.9 us; the launch traced here: 39.8 us
  Pallas kernels  39.1 us (98%)
  between operations  0.64 us (2%)
    pallas_call x1, Pallas kernels, shards(): pl.pallas_call(functools.partial(kernel, xs, zs, ys, forward_at, backward...  38.3 us
    pallas_call x1, Pallas kernels, shards(): pl.pallas_call(write_out, out_shape=tuple((jax.ShapeDtypeStruct(a.shape,...  0.82 us

profile of v3, /device:TPU:1, one launch (start us, length us, event | category | flops | bytes accessed | tf_op | source)
XLA Modules:
  0.0 39.8 jit_solution(15144119431862297810)
XLA Ops:
  0.6 38.3 %shard_map.75 = (bf16[32,2048]{1,0:T(8,128)(2,1)S(1)}, bf16[128,512]{1,0:T(8,128)(2,1)S(1)}, bf16[128,512]{1,0:T(8,128)(2,1)S(1)}, bf16[128,512]{1,0:T(8,128)(2,1)S(1)}) custom-call(bf16[128,512]{1,0:T(8,128)(2,1)} %q_hbm.1, bf16[128,512]{1,0:T(8,128)(2,1)} %k_hbm.1, bf16[128,512]{1,0:T(8,128)(2,1)} %v_hbm.1, bf16[32,2048]{1,0:T(8,128)(2,1)} %g_hbm.1), custom_call_target="tpu_custom_call" | custom-call | tf_op jit(solution)/shard_map/pallas_call | solution.py:331
  39.0 0.8 %shard_map.76 = (bf16[32,2048]{1,0:T(8,128)(2,1)}, bf16[128,512]{1,0:T(8,128)(2,1)}, bf16[128,512]{1,0:T(8,128)(2,1)}, bf16[128,512]{1,0:T(8,128)(2,1)}) custom-call(bf16[32,2048]{1,0:T(8,128)(2,1)S(1)} %get-tuple-element.8.refs_0_, bf16[128,512]{1,0:T(8,128)(2,1)S(1)} %get-tuple-element.9.refs_1_, bf16[128,512]{1,0:T(8,128)(2,1)S(1)} %get-tuple-element.10.refs_2_, ...), custom_call_target="tpu_custom_call" | custom-call | tf_op jit(solution)/shard_map/pallas_call | solution.py:353

commit v4 on v3

--- a/solution.py
+++ b/solution.py
@@ -24,7 +24,7 @@
 NN = (((1,), (0,)), ((), ()))
 NT = (((1,), (1,)), ((), ()))
 TN = (((0,), (0,)), ((), ()))
-G, CF, CR, OUT, TOT, BF, BR, AT = range(8)
+G, CF, CR, CF2, CR2, OUT, TOT, BF, BR, AT = range(10)
 
 
 def dot(a, b, dims=NN):
@@ -108,7 +108,7 @@
         pltpu.make_async_copy(src, dst, in_sem.at[i])
         for i, (src, dst) in enumerate(
             (
-                (k_hbm, k), (v_hbm, v), (g_hbm, g_in), (q_hbm, q),
+                (g_hbm, g_in), (k_hbm, k), (v_hbm, v), (q_hbm, q),
             )
         )
     ]
@@ -145,9 +145,14 @@
     def scaled(a):
         return (a.astype(F32) * factor).astype(BF16)
 
+    def to_sibling(own, sib, need, rest):
+        theirs, mine = aligned(1 - core, half), aligned(core, half)
+        send(own.at[theirs], sib.at[theirs], need, sibling)
+        send(own.at[mine], sib.at[mine], rest, sibling)
+
     def to_owners(own, sib, chip, which, places):
-        arrived(sib, which)
         mine = aligned(core, half)
+        arrived(sib.at[mine], which)
         chip[...] = (own[mine, :] + sib[mine, :]).astype(BF16)
         for i, place in enumerate(places):
             piece = chip.at[pl.ds(i * chunk, chunk)]
@@ -160,7 +165,7 @@
             def _(i=i, place=place):
                 line[place * chunk:(place + 1) * chunk, :] = chip[i * chunk:(i + 1) * chunk, :]
 
-    def own_chunk(scan, which, i, place, backward):
+    def sum_chunk(place, backward):
         arrived(line.at[pl.ds(0, (zs - 1) * chunk)], OUT)
         total = None
         for step in range(zs):
@@ -168,12 +173,13 @@
             piece = line[zz * chunk:(zz + 1) * chunk, :].astype(F32)
             part[zz * chunk:(zz + 1) * chunk, :] = jnp.zeros_like(piece) if total is None else total
             total = piece if total is None else total + piece
-        totals[aligned(x, chunk), :] = total
+        totals[aligned(x, chunk), :] = total.astype(BF16)
         for xx in range(xs):
             def pass_on(xx=xx):
                 send(totals.at[aligned(x, chunk)], totals.at[aligned(x, chunk)], TOT, device(xx, place, core))
 
             pl.when(xx < x if backward else xx > x)(pass_on)
+    def return_chunk(scan, which, i, place, backward):
         waits = (lambda xx: xs - 1 - xx) if backward else (lambda xx: xx)
         for xx in range(xs):
             if waits(xx):
@@ -182,14 +188,13 @@
                 def _(n=waits(xx)):
                     arrived(totals.at[pl.ds(0, n * chunk)], TOT)
 
-        base = jnp.zeros_like(total)
+        base = jnp.zeros((chunk, PAIR), F32)
         for xx in range(xs):
             counts = xx > x if backward else xx < x
-            base = base + jnp.where(counts, totals[xx * chunk:(xx + 1) * chunk, :], 0.0)
-        for zz in range(zs):
-            line_out[zz * chunk:(zz + 1) * chunk, :] = (part[zz * chunk:(zz + 1) * chunk, :] + base).astype(BF16)
+            base = base + jnp.where(counts, totals[xx * chunk:(xx + 1) * chunk, :].astype(F32), 0.0)
         home = pl.ds(pl.multiple_of(core * half + i * chunk, chunk), chunk)
         for zz in back_order:
+            line_out[zz * chunk:(zz + 1) * chunk, :] = (part[zz * chunk:(zz + 1) * chunk, :] + base).astype(BF16)
             piece = line_out.at[pl.ds(zz * chunk, chunk)]
             if zz == place:
                 send(piece, scan.at[home], which, sibling)
@@ -198,9 +203,13 @@
                 for cc in range(CORES):
                     send(piece, scan.at[home], which, device(x, zz, cc))
 
-    def own_one(scan, which, places, backward):
+    def sum_one(places, backward):
+        for place in places:
+            pl.when(z == place)(functools.partial(sum_chunk, place, backward))
+
+    def return_one(scan, which, places, backward):
         for i, place in enumerate(places):
-            pl.when(z == place)(functools.partial(own_chunk, scan, which, i, place, backward))
+            pl.when(z == place)(functools.partial(return_chunk, scan, which, i, place, backward))
 
     def came_back(scan, which, places):
         mine = among(z, places)
@@ -218,15 +227,15 @@
         return diagonal(jnp.concatenate(rows, axis=0)).astype(BF16)
 
     loads[0].wait()
-    loads[1].wait()
-    for p in range(pairs):
-        pair_state(own_f, p, k[:, columns(p)], v[:, columns(p)])
-    loads[2].wait()
     pl.semaphore_wait(barrier, greeted)
     for d in range(1, ys):
         to = (y + d) % ys
         send(g_in.at[:, aligned(to, width)], g.at[aligned(y, rows_y)], G, (seq, to))
-    send(own_f, sib_f, CF, sibling)
+    loads[1].wait()
+    loads[2].wait()
+    for p in range(pairs):
+        pair_state(own_f, p, k[:, columns(p)], v[:, columns(p)])
+    to_sibling(own_f, sib_f, CF, CF2)
     g[aligned(y, rows_y), :] = g_in[:, aligned(y, width)]
 
     causal = iota((2 * GROUP, GROUP), 0) % GROUP >= iota((2 * GROUP, GROUP), 1)
@@ -242,7 +251,7 @@
     arrived(g.at[pl.ds(0, (ys - 1) * rows_y)], G)
     for p in range(pairs):
         pair_state(own_r, p, q[:, columns(p)], scaled(g[:, columns(p)]))
-    send(own_r, sib_r, CR, sibling)
+    to_sibling(own_r, sib_r, CR, CR2)
     to_owners(own_r, sib_r, chip_r, CR, backward_at)
 
     for p in range(pairs):
@@ -255,10 +264,12 @@
         plain_t = jnp.where(causal_t, dot(k[:, c], q_two, NT), 0.0).astype(BF16)
         gv_l[:, c] = dot(plain_t, g_two)
 
-    own_one(scan_f, BF, forward_at, False)
-    own_one(scan_r, BR, backward_at, True)
+    sum_one(forward_at, False)
+    return_one(scan_f, BF, forward_at, False)
+    sum_one(backward_at, True)
 
     after = core.astype(F32)
+    arrived(sib_f.at[aligned(1 - core, half)], CF2)
     came_back(scan_f, BF, forward_at)
     for p in range(pairs):
         c = columns(p)
@@ -268,11 +279,13 @@
         to = (y + d) % ys
         send(attn_s.at[aligned(to, rows_y)], attn_r.at[:, aligned(y, width)], AT, (seq, to))
     attn_r[:, aligned(y, width)] = attn_s[aligned(y, rows_y), :]
+    return_one(scan_r, BR, backward_at, True)
     for p in range(pairs):
         c = columns(p)
         state = state_of(scan_f, sib_f, after, p)
         gq_s[:, c] = (gq_l[:, c] + dot(scaled(g[:, c]), state, NT)).astype(BF16)
 
+    arrived(sib_r.at[aligned(1 - core, half)], CR2)
     came_back(scan_r, BR, backward_at)
     for p in range(pairs):
         c = columns(p)
@@ -283,8 +296,8 @@
     arrived(attn_r.at[:, pl.ds(0, (ys - 1) * width)], AT)
 
     sent(g.at[pl.ds(0, (ys - 1) * rows_y)], G)
-    sent(own_f, CF)
-    sent(own_r, CR)
+    for which in (CF, CF2, CR, CR2):
+        sent(own_f.at[pl.ds(0, half)], which)
     sent(attn_r.at[:, pl.ds(0, (ys - 1) * width)], AT)
 
     @pl.when(jnp.logical_not(owner))
@@ -338,13 +351,13 @@
             state, state, state, state,
             chip, chip,
             line, pltpu.VMEM((zs * chunk, PAIR), F32), line,
-            pltpu.VMEM((xs * chunk, PAIR), F32),
+            pltpu.VMEM((xs * chunk, PAIR), BF16),
             scan, scan,
             wide, wide, wide, wide,
             block,
             pltpu.SemaphoreType.DMA((4,)),
-            pltpu.SemaphoreType.DMA((8,)),
-            pltpu.SemaphoreType.DMA((8,)),
+            pltpu.SemaphoreType.DMA((10,)),
+            pltpu.SemaphoreType.DMA((10,)),
         ],
         compiler_params=pltpu.CompilerParams(
             collective_id=0, has_side_effects=True, vmem_limit_bytes=32 * 2**20

time: 39.9 us -> 39.5 us (0.990)
  Pallas kernels: 39.1 us -> 38.7 us
    pallas_call x1, Pallas kernels: 38.3 us -> 37.9 us  [shards(): pl.pallas_call(functools.partial(kernel, xs, zs, ys, forward_at, backward...]
where the time goes in v4:
time: 39.5 us; the launch traced here: 39.3 us
  Pallas kernels  38.7 us (98%)
  between operations  0.64 us (2%)
    pallas_call x1, Pallas kernels, shards(): pl.pallas_call(functools.partial(kernel, xs, zs, ys, forward_at, backward...  37.9 us
    pallas_call x1, Pallas kernels, shards(): pl.pallas_call(write_out, out_shape=tuple((jax.ShapeDtypeStruct(a.shape,...  0.82 us

profile of v4, /device:TPU:1, one launch (start us, length us, event | category | flops | bytes accessed | tf_op | source)
XLA Modules:
  0.0 39.3 jit_solution(13689190855328628468)
XLA Ops:
  0.6 37.9 %shard_map.75 = (bf16[32,2048]{1,0:T(8,128)(2,1)S(1)}, bf16[128,512]{1,0:T(8,128)(2,1)S(1)}, bf16[128,512]{1,0:T(8,128)(2,1)S(1)}, bf16[128,512]{1,0:T(8,128)(2,1)S(1)}) custom-call(bf16[128,512]{1,0:T(8,128)(2,1)} %q_hbm.1, bf16[128,512]{1,0:T(8,128)(2,1)} %k_hbm.1, bf16[128,512]{1,0:T(8,128)(2,1)} %v_hbm.1, bf16[32,2048]{1,0:T(8,128)(2,1)} %g_hbm.1), custom_call_target="tpu_custom_call" | custom-call | tf_op jit(solution)/shard_map/pallas_call | solution.py:344
  38.5 0.8 %shard_map.76 = (bf16[32,2048]{1,0:T(8,128)(2,1)}, bf16[128,512]{1,0:T(8,128)(2,1)}, bf16[128,512]{1,0:T(8,128)(2,1)}, bf16[128,512]{1,0:T(8,128)(2,1)}) custom-call(bf16[32,2048]{1,0:T(8,128)(2,1)S(1)} %get-tuple-element.8.refs_0_, bf16[128,512]{1,0:T(8,128)(2,1)S(1)} %get-tuple-element.9.refs_1_, bf16[128,512]{1,0:T(8,128)(2,1)S(1)} %get-tuple-element.10.refs_2_, ...), custom_call_target="tpu_custom_call" | custom-call | tf_op jit(solution)/shard_map/pallas_call | solution.py:366

commit v5 on v4

--- a/solution.py
+++ b/solution.py
@@ -173,7 +173,7 @@
             piece = line[zz * chunk:(zz + 1) * chunk, :].astype(F32)
             part[zz * chunk:(zz + 1) * chunk, :] = jnp.zeros_like(piece) if total is None else total
             total = piece if total is None else total + piece
-        totals[aligned(x, chunk), :] = total.astype(BF16)
+        totals[aligned(x, chunk), :] = total
         for xx in range(xs):
             def pass_on(xx=xx):
                 send(totals.at[aligned(x, chunk)], totals.at[aligned(x, chunk)], TOT, device(xx, place, core))
@@ -191,7 +191,7 @@
         base = jnp.zeros((chunk, PAIR), F32)
         for xx in range(xs):
             counts = xx > x if backward else xx < x
-            base = base + jnp.where(counts, totals[xx * chunk:(xx + 1) * chunk, :].astype(F32), 0.0)
+            base = base + jnp.where(counts, totals[xx * chunk:(xx + 1) * chunk, :], 0.0)
         home = pl.ds(pl.multiple_of(core * half + i * chunk, chunk), chunk)
         for zz in back_order:
             line_out[zz * chunk:(zz + 1) * chunk, :] = (part[zz * chunk:(zz + 1) * chunk, :] + base).astype(BF16)
@@ -351,7 +351,7 @@
             state, state, state, state,
             chip, chip,
             line, pltpu.VMEM((zs * chunk, PAIR), F32), line,
-            pltpu.VMEM((xs * chunk, PAIR), BF16),
+            pltpu.VMEM((xs * chunk, PAIR), F32),
             scan, scan,
             wide, wide, wide, wide,
             block,

time: 39.5 us -> 39.4 us (level)
  no operation moved by 1% of the time
where the time goes in v5:
time: 39.4 us; the launch traced here: 39.3 us
  Pallas kernels  38.6 us (98%)
  between operations  0.64 us (2%)
    pallas_call x1, Pallas kernels, shards(): pl.pallas_call(functools.partial(kernel, xs, zs, ys, forward_at, backward...  37.8 us
    pallas_call x1, Pallas kernels, shards(): pl.pallas_call(write_out, out_shape=tuple((jax.ShapeDtypeStruct(a.shape,...  0.82 us

profile of v5, /device:TPU:1, one launch (start us, length us, event | category | flops | bytes accessed | tf_op | source)
XLA Modules:
  0.0 39.3 jit_solution(3655875969378166616)
XLA Ops:
  0.6 37.8 %shard_map.75 = (bf16[32,2048]{1,0:T(8,128)(2,1)S(1)}, bf16[128,512]{1,0:T(8,128)(2,1)S(1)}, bf16[128,512]{1,0:T(8,128)(2,1)S(1)}, bf16[128,512]{1,0:T(8,128)(2,1)S(1)}) custom-call(bf16[128,512]{1,0:T(8,128)(2,1)} %q_hbm.1, bf16[128,512]{1,0:T(8,128)(2,1)} %k_hbm.1, bf16[128,512]{1,0:T(8,128)(2,1)} %v_hbm.1, bf16[32,2048]{1,0:T(8,128)(2,1)} %g_hbm.1), custom_call_target="tpu_custom_call" | custom-call | tf_op jit(solution)/shard_map/pallas_call | solution.py:344
  38.5 0.8 %shard_map.76 = (bf16[32,2048]{1,0:T(8,128)(2,1)}, bf16[128,512]{1,0:T(8,128)(2,1)}, bf16[128,512]{1,0:T(8,128)(2,1)}, bf16[128,512]{1,0:T(8,128)(2,1)}) custom-call(bf16[32,2048]{1,0:T(8,128)(2,1)S(1)} %get-tuple-element.8.refs_0_, bf16[128,512]{1,0:T(8,128)(2,1)S(1)} %get-tuple-element.9.refs_1_, bf16[128,512]{1,0:T(8,128)(2,1)S(1)} %get-tuple-element.10.refs_2_, ...), custom_call_target="tpu_custom_call" | custom-call | tf_op jit(solution)/shard_map/pallas_call | solution.py:366

commit v6 on v5

--- a/solution.py
+++ b/solution.py
@@ -275,9 +275,12 @@
         c = columns(p)
         state = state_of(scan_f, sib_f, after, p)
         attn_s[:, c] = (attn_l[:, c] + dot(scaled(q[:, c]), state)).astype(BF16)
-    for d in range(1, ys):
-        to = (y + d) % ys
-        send(attn_s.at[aligned(to, rows_y)], attn_r.at[:, aligned(y, width)], AT, (seq, to))
+        if p % 2:
+            first = (p - 1) * PAIR
+            there = pl.ds(pl.multiple_of(y * width + first, PAIR), 2 * PAIR)
+            for d in range(1, ys):
+                to = (y + d) % ys
+                send(attn_s.at[aligned(to, rows_y), pl.ds(first, 2 * PAIR)], attn_r.at[:, there], AT, (seq, to))
     attn_r[:, aligned(y, width)] = attn_s[aligned(y, rows_y), :]
     return_one(scan_r, BR, backward_at, True)
     for p in range(pairs):

time: 39.4 us -> 39.4 us (level)
  no operation moved by 1% of the time
where the time goes in v6:
time: 39.4 us; the launch traced here: 39.3 us
  Pallas kernels  38.7 us (98%)
  between operations  0.64 us (2%)
    pallas_call x1, Pallas kernels, shards(): pl.pallas_call(functools.partial(kernel, xs, zs, ys, forward_at, backward...  37.8 us
    pallas_call x1, Pallas kernels, shards(): pl.pallas_call(write_out, out_shape=tuple((jax.ShapeDtypeStruct(a.shape,...  0.82 us

profile of v6, /device:TPU:1, one launch (start us, length us, event | category | flops | bytes accessed | tf_op | source)
XLA Modules:
  0.0 39.3 jit_solution(12861240519260069651)
XLA Ops:
  0.6 37.8 %shard_map.75 = (bf16[32,2048]{1,0:T(8,128)(2,1)S(1)}, bf16[128,512]{1,0:T(8,128)(2,1)S(1)}, bf16[128,512]{1,0:T(8,128)(2,1)S(1)}, bf16[128,512]{1,0:T(8,128)(2,1)S(1)}) custom-call(bf16[128,512]{1,0:T(8,128)(2,1)} %q_hbm.1, bf16[128,512]{1,0:T(8,128)(2,1)} %k_hbm.1, bf16[128,512]{1,0:T(8,128)(2,1)} %v_hbm.1, bf16[32,2048]{1,0:T(8,128)(2,1)} %g_hbm.1), custom_call_target="tpu_custom_call" | custom-call | tf_op jit(solution)/shard_map/pallas_call | solution.py:347
  38.5 0.8 %shard_map.76 = (bf16[32,2048]{1,0:T(8,128)(2,1)}, bf16[128,512]{1,0:T(8,128)(2,1)}, bf16[128,512]{1,0:T(8,128)(2,1)}, bf16[128,512]{1,0:T(8,128)(2,1)}) custom-call(bf16[32,2048]{1,0:T(8,128)(2,1)S(1)} %get-tuple-element.8.refs_0_, bf16[128,512]{1,0:T(8,128)(2,1)S(1)} %get-tuple-element.9.refs_1_, bf16[128,512]{1,0:T(8,128)(2,1)S(1)} %get-tuple-element.10.refs_2_, ...), custom_call_target="tpu_custom_call" | custom-call | tf_op jit(solution)/shard_map/pallas_call | solution.py:369
